TPU v7x, 256 devices: a whole 4x4x8 slice. The times are simulated.
256 devices in a mesh: dp: 32 (over z, y), mp: 8 (over x, core).
Axes of the slice: x: 4, y: 4, z: 8, core: 2. Of those that a mesh axis runs over, the one named last changes fastest.
Arguments:
- loaded: bfloat16 [5, 8192, 8192], P(None, ('dp', 'mp')), may hold values from -6 to 6
- row_plan: int32 [8192], P(('dp', 'mp')), may hold values from 0 to 8191, as said below
- lengths: int32 [3], replicated, may hold values from 1 to 4096, 8192 in all
- se_filter: bfloat16 [7, 512], P(None, 'mp'), may hold values from -2 to 2
- mr_filter: bfloat16 [128, 512], P(None, 'mp'), may hold values from -0.5 to 0.5
- grad_out: bfloat16 [8192, 8192], P('dp', 'mp'), may hold values from -6 to 6
Outputs:
- grad_loaded: bfloat16 [5, 8192, 8192], P(None, ('dp', 'mp'))
- se_grad: float32 [7, 512], P(None, 'mp')
- mr_grad: float32 [128, 512], P(None, 'mp')
Inputs may be any that keep to these rules, and one draw needn't show every extreme that they name: row_plan is a permutation of the 8192 packed rows; of the 256 loaded rows of one dp index at most 16 go to the packed rows k * 256 to (k + 1) * 256 - 1 of any one k, and exactly 16 to some k.
All inputs are finite; a program needn't handle non-finite values.
Results may differ from a plain program's by a relative error of at most 0.0075.
Values may be sent and summed in bfloat16 or wider, within the bound.
No kernel may reach another device: no remote copies, remote signals or barrier semaphores. Data moves between devices by JAX's collectives and lax.ppermute only.
A program may use at most 128 MiB of HBM per device.

v0:
```python
import jax
import jax.numpy as jnp
from jax import lax
from jax.sharding import PartitionSpec as P


def shifted(shard, axis, by):
    length = lax.axis_size(axis)
    pairs = [(i, i + by) for i in range(length) if 0 <= i + by < length]
    return lax.ppermute(shard, axis, pairs)


def sequence_starts(row_ids, lengths):
    finish = jnp.cumsum(lengths)
    passed = finish[None, :] <= row_ids[:, None]
    return jnp.sum(jnp.where(passed, lengths[None, :], 0), axis=1)


def band_tiles(taps_by_group, causal):
    tap_count, group_count = taps_by_group.shape
    columns = jnp.transpose(taps_by_group)
    if causal:
        head_row = jnp.concatenate(
            [
                jnp.zeros((group_count, 1), taps_by_group.dtype),
                columns[:, ::-1],
                jnp.zeros((group_count, tap_count), taps_by_group.dtype),
            ],
            axis=1,
        )
    else:
        head_row = jnp.concatenate(
            [columns, jnp.zeros((group_count, tap_count + 1), taps_by_group.dtype)], axis=1
        )
    repeated = jnp.tile(head_row, (1, tap_count))
    return repeated[:, : 2 * tap_count * tap_count].reshape(group_count, tap_count, 2 * tap_count)


def lag_sums(blocks):
    group_count, tap_count, span_width = blocks.shape
    flat_rows = blocks.reshape(group_count, tap_count * span_width)
    flat_rows = jnp.concatenate(
        [flat_rows, jnp.zeros((group_count, tap_count), blocks.dtype)], axis=1
    )
    skewed = flat_rows.reshape(group_count, tap_count, span_width + 1)
    return jnp.transpose(jnp.sum(skewed[:, :, 1 : tap_count + 1], axis=1)[:, ::-1])


def short_forward(padded, weights, starts, anchor, margin):
    out_rows = padded.shape[0] - margin
    targets = anchor + jnp.arange(out_rows, dtype=jnp.int32)
    result = jnp.zeros((out_rows, padded.shape[1]), jnp.float32)
    for step_lag in range(weights.shape[0]):
        source = padded[margin - step_lag : margin - step_lag + out_rows].astype(jnp.float32)
        allowed = (targets - step_lag >= starts)[:, None]
        result = result + jnp.where(allowed, source * weights[step_lag][None, :], 0.0)
    return result


def short_backward(extended, weights, later_starts, anchor, out_rows):
    sources = anchor + jnp.arange(out_rows, dtype=jnp.int32)
    result = jnp.zeros((out_rows, extended.shape[1]), jnp.float32)
    for step_lag in range(weights.shape[0]):
        later = extended[step_lag : step_lag + out_rows].astype(jnp.float32)
        allowed = (sources >= later_starts[step_lag : step_lag + out_rows])[:, None]
        result = result + jnp.where(allowed, later * weights[step_lag][None, :], 0.0)
    return result


def short_grads(grad_rows, padded, starts, anchor, margin, tap_count, group_count):
    out_rows = grad_rows.shape[0]
    channels = grad_rows.shape[1]
    targets = anchor + jnp.arange(out_rows, dtype=jnp.int32)
    outcome = []
    for step_lag in range(tap_count):
        source = padded[margin - step_lag : margin - step_lag + out_rows].astype(jnp.float32)
        allowed = (targets - step_lag >= starts)[:, None]
        terms = jnp.where(allowed, grad_rows.astype(jnp.float32) * source, 0.0)
        outcome.append(
            jnp.sum(terms.reshape(out_rows, group_count, channels // group_count), axis=(0, 2))
        )
    return jnp.stack(outcome)


def long_forward(extended, tiles, starts, anchor):
    group_count, tap_count, span_width = tiles.shape
    channels = extended.shape[1]
    per_group = channels // group_count
    slab_count = (extended.shape[0] - tap_count) // tap_count

    def one_slab(slab_index):
        slab_start = slab_index * tap_count
        window = lax.dynamic_slice_in_dim(extended, slab_start, span_width, 0).reshape(
            span_width, group_count, per_group
        )
        row_starts = lax.dynamic_slice_in_dim(starts, slab_start, tap_count, 0)
        sources = anchor + slab_start - tap_count + jnp.arange(span_width, dtype=jnp.int32)
        keep_mask = (sources[None, :] >= row_starts[:, None]).astype(tiles.dtype)
        mixed_rows = jnp.einsum(
            "gim,mgc->igc",
            tiles * keep_mask[None, :, :],
            window,
            preferred_element_type=jnp.float32,
        )
        return mixed_rows.reshape(tap_count, channels)

    return lax.map(one_slab, jnp.arange(slab_count, dtype=jnp.int32)).reshape(
        slab_count * tap_count, channels
    )


def long_backward(extended, tiles, later_starts, anchor):
    group_count, tap_count, span_width = tiles.shape
    channels = extended.shape[1]
    per_group = channels // group_count
    slab_count = (extended.shape[0] - tap_count) // tap_count

    def one_slab(slab_index):
        slab_start = slab_index * tap_count
        window = lax.dynamic_slice_in_dim(extended, slab_start, span_width, 0).reshape(
            span_width, group_count, per_group
        )
        their_starts = lax.dynamic_slice_in_dim(later_starts, slab_start, span_width, 0)
        sources = anchor + slab_start + jnp.arange(tap_count, dtype=jnp.int32)
        keep_mask = (sources[:, None] >= their_starts[None, :]).astype(tiles.dtype)
        mixed_rows = jnp.einsum(
            "gim,mgc->igc",
            tiles * keep_mask[None, :, :],
            window,
            preferred_element_type=jnp.float32,
        )
        return mixed_rows.reshape(tap_count, channels)

    return lax.map(one_slab, jnp.arange(slab_count, dtype=jnp.int32)).reshape(
        slab_count * tap_count, channels
    )


def long_grads(grad_rows, extended, starts, anchor, tap_count, group_count):
    channels = grad_rows.shape[1]
    per_group = channels // group_count
    span_width = 2 * tap_count
    slab_count = grad_rows.shape[0] // tap_count

    def one_slab(carry, slab_index):
        slab_start = slab_index * tap_count
        window = lax.dynamic_slice_in_dim(extended, slab_start, span_width, 0).reshape(
            span_width, group_count, per_group
        )
        rows_here = lax.dynamic_slice_in_dim(grad_rows, slab_start, tap_count, 0).reshape(
            tap_count, group_count, per_group
        )
        row_starts = lax.dynamic_slice_in_dim(starts, slab_start, tap_count, 0)
        sources = anchor + slab_start - tap_count + jnp.arange(span_width, dtype=jnp.int32)
        keep_mask = (sources[None, :] >= row_starts[:, None]).astype(jnp.float32)
        grid = jnp.einsum("igc,mgc->gim", rows_here, window, preferred_element_type=jnp.float32)
        return (carry + grid * keep_mask[None, :, :], None)

    initial = jnp.zeros((group_count, tap_count, span_width), jnp.float32)
    summed, unused = lax.scan(one_slab, initial, jnp.arange(slab_count, dtype=jnp.int32))
    return lag_sums(summed)


def on_device(loaded, row_plan, lengths, se_filter, mr_filter, grad_out):
    shards = lax.axis_size("dp")
    dp_index = lax.axis_index("dp")
    local_rows = grad_out.shape[0]
    channels = grad_out.shape[1]
    group_count = se_filter.shape[1]
    per_group = channels // group_count
    tap_count = mr_filter.shape[0]
    short_taps = se_filter.shape[0]
    margin = 8
    capacity = 2 * local_rows // shards
    anchor = dp_index * local_rows
    full_plan = lax.all_gather(row_plan, ("dp", "mp"), axis=0, tiled=True)
    group_plan = lax.dynamic_slice_in_dim(full_plan, anchor, local_rows, 0)
    target = group_plan // local_rows
    matches = (target[:, None] == jnp.arange(shards, dtype=jnp.int32)[None, :]).astype(jnp.int32)
    earlier = jnp.cumsum(matches, axis=0) - matches
    packed_at = target * capacity + jnp.sum(earlier * matches, axis=1)
    every_plan = full_plan.reshape(shards, local_rows)
    arriving = (every_plan // local_rows == dp_index).astype(jnp.int32)
    arrival_rank = jnp.cumsum(arriving, axis=1) - arriving
    sent_from = jnp.arange(shards, dtype=jnp.int32)[:, None] * capacity + arrival_rank
    landing = jnp.where(arriving == 1, every_plan % local_rows, local_rows)
    source_of = (
        jnp.zeros((local_rows,), jnp.int32)
        .at[landing.reshape(-1)]
        .set(sent_from.reshape(-1), mode="drop")
    )
    columns = lax.all_to_all(loaded, "mp", split_axis=2, concat_axis=1, tiled=True)
    parcels = (
        jnp.zeros((columns.shape[0], shards * capacity, channels), jnp.bfloat16)
        .at[:, packed_at, :]
        .set(columns)
    )
    received = lax.all_to_all(parcels, "dp", split_axis=1, concat_axis=1, tiled=True)
    context = received[:, source_of, :]
    gate_one = context[0]
    key_one = context[1]
    value_one = context[2]
    gate_two = context[3]
    key_two = context[4]
    inner_one = (key_one.astype(jnp.float32) * value_one.astype(jnp.float32)).astype(jnp.bfloat16)
    here_rows = anchor + jnp.arange(local_rows, dtype=jnp.int32)
    starts_here = sequence_starts(here_rows, lengths)
    later_rows = anchor + jnp.arange(local_rows + tap_count, dtype=jnp.int32)
    later_starts = sequence_starts(later_rows, lengths)
    short_weights = jnp.repeat(se_filter.astype(jnp.float32), per_group, axis=1)
    forward_tiles = band_tiles(mr_filter, True)
    backward_tiles = band_tiles(mr_filter, False)
    inner_rim = shifted(inner_one[local_rows - margin :], "dp", 1)
    padded_one = jnp.concatenate([inner_rim, inner_one], axis=0)
    short_mix = short_forward(padded_one, short_weights, starts_here, anchor, margin)
    middle = (gate_one.astype(jnp.float32) * short_mix).astype(jnp.bfloat16)
    inner_two = (key_two.astype(jnp.float32) * middle.astype(jnp.float32)).astype(jnp.bfloat16)
    inner_rim_two = shifted(inner_two[local_rows - tap_count :], "dp", 1)
    padded_two = jnp.concatenate([inner_rim_two, inner_two], axis=0)
    long_mix = long_forward(padded_two, forward_tiles, starts_here, anchor)
    cotangent = grad_out.astype(jnp.float32)
    grad_mix_two = (cotangent * gate_two.astype(jnp.float32)).astype(jnp.bfloat16)
    grad_gate_two = (cotangent * long_mix).astype(jnp.bfloat16)
    back_rim = shifted(grad_mix_two[:tap_count], "dp", -1)
    grad_inner_two = long_backward(
        jnp.concatenate([grad_mix_two, back_rim], axis=0), backward_tiles, later_starts, anchor
    )
    grad_key_two = (grad_inner_two * middle.astype(jnp.float32)).astype(jnp.bfloat16)
    grad_middle = grad_inner_two * key_two.astype(jnp.float32)
    grad_gate_one = (grad_middle * short_mix).astype(jnp.bfloat16)
    grad_mix_one = (grad_middle * gate_one.astype(jnp.float32)).astype(jnp.bfloat16)
    short_back = shifted(grad_mix_one[:margin], "dp", -1)
    grad_inner_one = short_backward(
        jnp.concatenate([grad_mix_one, short_back], axis=0),
        short_weights,
        later_starts[: local_rows + margin],
        anchor,
        local_rows,
    ).astype(jnp.bfloat16)
    long_part = long_grads(grad_mix_two, padded_two, starts_here, anchor, tap_count, group_count)
    short_part = short_grads(
        grad_mix_one, padded_one, starts_here, anchor, margin, short_taps, group_count
    )
    short_total, long_total = lax.psum((short_part, long_part), "dp")
    unit_scale = (local_rows * shards * per_group) ** (-0.5)
    grad_key_one = (grad_inner_one.astype(jnp.float32) * value_one.astype(jnp.float32)).astype(
        jnp.bfloat16
    )
    grad_value_one = (grad_inner_one.astype(jnp.float32) * key_one.astype(jnp.float32)).astype(
        jnp.bfloat16
    )
    returning = jnp.stack(
        [grad_gate_one, grad_key_one, grad_value_one, grad_gate_two, grad_key_two]
    )
    outbound = (
        jnp.zeros((returning.shape[0], shards * capacity, channels), jnp.bfloat16)
        .at[:, source_of, :]
        .set(returning)
    )
    returned = lax.all_to_all(outbound, "dp", split_axis=1, concat_axis=1, tiled=True)
    own_rows = returned[:, packed_at, :]
    restored = lax.all_to_all(own_rows, "mp", split_axis=1, concat_axis=2, tiled=True)
    return (restored, short_total * unit_scale, long_total * unit_scale)


def solution(mesh):
    placed = (
        P(None, ("dp", "mp"), None),
        P(("dp", "mp")),
        P(),
        P(None, "mp"),
        P(None, "mp"),
        P("dp", "mp"),
    )
    return jax.shard_map(
        on_device,
        mesh=mesh,
        in_specs=placed,
        out_specs=(P(None, ("dp", "mp"), None), P(None, "mp"), P(None, "mp")),
        check_vma=False,
    )
```

profile of v0, /device:TPU:4, one launch (start us, length us, event | category | flops | bytes accessed | tf_op | source)
XLA Modules:
  0.0 939.2 jit_solution(16717614205049255059)
XLA Ops:
  0.6 14.7 %copy.86 = bf16[5,32,8192]{1,0,2:T(8,128)(2,1)} copy(bf16[5,32,8192]{2,1,0:T(8,128)(2,1)} %param.12) | data formatting | bytes 5242880 | tf_op args[0]
  15.4 13.7 %reshape.441 = bf16[8,2,81920]{2,1,0:T(2,128)(2,1)} reshape(bf16[8192,5,32]{2,1,0:T(8,128)(2,1)} %bitcast.199) | data formatting | bytes 5242880
  29.1 5.9 all-to-all-start
  35.3 99.3 %all-reduce.2 = s32[8192]{0:T(1024)S(1)} all-reduce(s32[8192]{0:T(1024)S(1)} %dynamic-update-slice), channel_id=1, replica_groups=mesh['dp'=32,'mp'=8] {'dp','mp'}, use_global_device_ids=true, to_apply=%add.2 | all-reduce | flops 8192 | bytes 65536
  135.8 11.8 %reshape.442 = bf16[8192,5,32]{2,1,0:T(8,128)(2,1)} reshape(bf16[8,2,81920]{2,1,0:T(2,128)(2,1)S(1)} %all-to-all-done) | data formatting | bytes 5242880
  147.7 19.8 %copy.87 = bf16[5,8,32,1024]{3,0,2,1:T(8,128)(2,1)} copy(bf16[5,8,32,1024]{2,0,3,1:T(8,128)(2,1)} %bitcast.198) | data formatting | bytes 5242880 | tf_op jit(solution)/shard_map/all_to_all | solution.py:192
  167.4 4.3 broadcast.301.clone
  171.7 33.6 %scatter_fusion = bf16[5,512,1024]{2,0,1:T(8,128)(2,1)} fusion(bf16[5,512,1024]{2,0,1:T(8,128)(2,1)} %broadcast.301.clone, s32[256]{0:T(256)S(1)} %compare_select_fusion.1, bf16[256,5,1024]{2,1,0:T(8,128)(2,1)} %bitcast.211), kind=kCustom, calls=%fused_computation.3 | custom fusion | bytes 7865344 | tf_op jit(solution)/shard_map/scatter | solution.py:196
  205.3 6.6 all-to-all-start.1
  213.3 3.2 tile.8
  216.5 10.8 %tile.9 = bf16[64,32896]{1,0:T(8,128)(2,1)} reshape(bf16[64,128,257]{2,1,0:T(8,128)(2,1)} %tile.8) | data formatting | bytes 8421376 | tf_op jit(solution)/shard_map/tile | solution.py:35
  227.3 2.2 slice-done
  229.5 3.0 copy.130
  233.9 3.2 tile.20
  237.1 10.8 %tile.21 = bf16[64,32896]{1,0:T(8,128)(2,1)} reshape(bf16[64,128,257]{2,1,0:T(8,128)(2,1)} %tile.20) | data formatting | bytes 8421376 | tf_op jit(solution)/shard_map/tile | solution.py:35
  247.9 2.2 slice-done.1
  250.1 3.0 copy.131
  253.1 30.4 %scatter_custom_fusion = s32[256]{0:T(256)S(1)} fusion(s32[8192]{0:T(1024)S(1)} %get-tuple-element.414, s32[8192]{0:T(1024)S(1)} %get-tuple-element.413, s32[]{:T(128)} %copy.203), kind=kCustom, calls=%fused_computation.206 | custom fusion | bytes 1028 | tf_op jit(solution)/shard_map/scatter | solution.py:190
  285.1 117.5 %all-to-all-done.1 = bf16[5,512,1024]{2,0,1:T(8,128)(2,1)} async-done(((bf16[5,512,1024]{2,0,1:T(8,128)(2,1)}), bf16[5,512,1024]{2,0,1:T(8,128)(2,1)}, u32[]{:S(2)}, u32[]{:S(2)}) %all-to-all-start.1) | async-done | bytes 5242912 | tf_op jit(solution)/shard_map/all_to_all | solution.py:198
  402.5 6.2 gather_fusion
  408.7 14.2 %slice_convert_fusion.1 = (f32[1,256,1024]{2,0,1:T(1,128)S(1)}, bf16[1,256,1024]{2,0,1:T(2,128)(2,1)S(1)}, bf16[1,256,1024]{2,0,1:T(2,128)(2,1)S(1)}, f32[1,256,1024]{2,0,1:T(1,128)S(1)}, bf16[1,256,1024]{2,0,1:T(2,128)(2,1)}) fusion(bf16[5,256,1024]{2,0,1:T(8,128)(2,1)} %bitcast.207), kind=kLoop, calls=%fused_computation.93 | loop fusion | flops 524288 | bytes 6291456 | tf_op jit(solution)/shard_map/convert_element_type | solution.py:205
  423.2 1.3 collective-permute-start
  425.0 4.7 collective-permute-start.1
  429.8 2.6 collective-permute-done
  433.0 13.2 %while.38 = (s32[]{:T(128)}, f32[2,128,1024]{1,2,0:T(8,128)}, s32[2]{0:T(128)}, bf16[384,1024]{1,0:T(8,128)(2,1)S(1)}, s32[]{:T(128)}, /*index=5*/s32[384]{0:T(512)S(1)}, bf16[64,128,256]{2,1,0:T(8,128)(2,1)}, s32[1]{0:T(128)}) while((s32[]{:T(128)}, f32[2,128,1024]{1,2,0:T(8,128)}, s32[2]{0:T(128)}, ...), condition=%wide.region_10.11_spmd.clone, body=%wide.region_9.10_spmd.sunk.clone | while | flops 69271688 | bytes 8524455 | solution.py:134
  435.4 3.4 fusion.106
  439.6 1.3 dynamic_slice.90
  442.0 3.4 fusion.106
  446.2 1.6 copy.90
  447.9 5.9 fusion.23
  454.3 1.6 collective-permute-start.3
  456.0 1.9 fusion.43
  458.0 1.3 collective-permute-start.2
  459.4 5.6 collective-permute-done.2
  465.0 2.8 fusion.52
  468.2 1.5 copy-done.8
  470.1 11.9 %while.39 = (s32[]{:T(128)}, f32[2,128,1024]{2,1,0:T(8,128)}, s32[2]{0:T(128)S(1)}, bf16[384,1024]{0,1:T(8,128)(2,1)S(1)}, s32[]{:T(128)}, /*index=5*/s32[256]{0:T(256)S(1)}, bf16[64,128,256]{2,1,0:T(8,128)(2,1)}, s32[1]{0:T(128)}) while((s32[]{:T(128)}, f32[2,128,1024]{2,1,0:T(8,128)}, s32[2]{0:T(128)S(1)}, ...), condition=%wide.region_13.14_spmd.clone, body=%wide.region_12.13_spmd.sunk.clone | while | flops 69271816 | bytes 8523980 | solution.py:107
  471.6 3.4 fusion.109
  477.5 3.4 fusion.109
  482.0 2.3 bitcast_dynamic-update-slice_fusion.1
  484.3 1.9 bitcast_dynamic-update-slice_fusion
  486.2 5.3 copy.95
  491.4 4.3 broadcast.301
  495.7 33.5 %scatter_fusion.1 = bf16[5,512,1024]{2,0,1:T(8,128)(2,1)} fusion(bf16[5,512,1024]{2,0,1:T(8,128)(2,1)} %broadcast.301, s32[256]{0:T(256)S(1)} %compare_select_fusion.2, bf16[256,5,1024]{2,1,0:T(8,128)(2,1)} %copy.95), kind=kCustom, calls=%fused_computation.4 | custom fusion | bytes 7865344 | tf_op jit(solution)/shard_map/scatter | solution.py:258
  529.2 15.3 %all-to-all-start.2 = ((bf16[5,512,1024]{2,0,1:T(8,128)(2,1)}), bf16[5,512,1024]{2,0,1:T(8,128)(2,1)}, u32[]{:S(2)}, u32[]{:S(2)}) async-start(bf16[5,512,1024]{2,0,1:T(8,128)(2,1)} %scatter_fusion.1), calls=%async_computation.2 | async-start | bytes 16777216 | tf_op jit(solution)/shard_map/all_to_all | solution.py:260
  544.6 1.9 copy_convert_fusion
  546.5 1.5 copy.97
  548.0 1.6 copy.98
  549.6 5.6 convert_convert_fusion
  556.4 2.6 copy.99
  559.0 1.8 select_reduce_fusion
  562.2 161.6 %all-to-all-done.2 = bf16[5,512,1024]{2,0,1:T(8,128)(2,1)} async-done(((bf16[5,512,1024]{2,0,1:T(8,128)(2,1)}), bf16[5,512,1024]{2,0,1:T(8,128)(2,1)}, u32[]{:S(2)}, u32[]{:S(2)}) %all-to-all-start.2) | async-done | bytes 5242912 | tf_op jit(solution)/shard_map/all_to_all | solution.py:260
  723.8 6.2 gather_fusion.1
  730.0 11.7 %all-to-all-start.3 = ((bf16[5,256,1024]{2,0,1:T(8,128)(2,1)}), bf16[5,256,1024]{2,0,1:T(8,128)(2,1)}, u32[]{:S(2)}, u32[]{:S(2)}) async-start(bf16[5,256,1024]{2,0,1:T(8,128)(2,1)} %bitcast.212), calls=%async_computation.3 | async-start | bytes 8388608 | tf_op jit(solution)/shard_map/all_to_all | solution.py:262
  741.7 16.0 %while.40 = (s32[]{:T(128)}, f32[64,128,256]{2,1,0:T(8,128)}, s32[2]{0:T(128)S(1)}, bf16[256,1024]{1,0:T(8,128)(2,1)S(1)}, bf16[384,1024]{0,1:T(8,128)(2,1)S(1)}, /*index=5*/s32[]{:T(128)}, s32[256]{0:T(256)S(1)}, s32[1]{0:T(128)}) while((s32[]{:T(128)}, f32[64,128,256]{2,1,0:T(8,128)}, s32[2]{0:T(128)S(1)}, ...), condition=%wide.region_31.32_spmd.clone.clone, body=%wide.region_30.31_spmd.clone.sunk.clone | while | flops 73466120 | bytes 19926744 | solution.py:160
  743.4 4.6 select_add_fusion.3
  749.7 8.0 select_add_fusion.3
  757.7 8.1 copy.132
  765.8 3.8 concatenate.27
  769.5 14.1 %reshape.378 = f32[64,128,257]{2,1,0:T(8,128)} reshape(f32[64,32896]{1,0:T(8,128)} %concatenate.27) | data formatting | bytes 16842752 | tf_op jit(solution)/shard_map/reshape | solution.py:45
  783.7 4.5 slice_reduce_fusion
  788.3 142.4 %all-reduce.3 = (f32[7,64]{1,0:T(8,128)S(1)}, f32[128,64]{0,1:T(8,128)S(1)}) all-reduce(f32[7,64]{1,0:T(8,128)S(1)} %stack.55, f32[128,64]{0,1:T(8,128)S(1)} %bitcast.220), channel_id=1, replica_groups=mesh['dp'=32,'mp'=8] {'dp'}, use_global_device_ids=true, to_apply=%region_29.30 | all-reduce | flops 8640 | bytes 69120 | tf_op jit(solution)/shard_map/psum | solution.py:244
  932.0 3.9 copy.96
  935.9 3.1 all_to_all.41
  (190 shorter events, 21.7 us)
Async XLA Ops:
  29.1 5.9 copy-start.25
  29.1 106.7 %all-to-all-start = ((bf16[8,2,81920]{2,1,0:T(2,128)(2,1)}), bf16[8,2,81920]{2,1,0:T(2,128)(2,1)S(1)}, u32[]{:S(2)}, u32[]{:S(2)}) async-start(bf16[8,2,81920]{2,1,0:T(2,128)(2,1)} %reshape.441), calls=%async_computation | async-start | bytes 5242880 | tf_op jit(solution)/shard_map/all_to_all | solution.py:192
  205.3 7.7 copy-start.24
  205.3 7.9 copy-start.10
  205.3 197.2 %all-to-all-start.1 = ((bf16[5,512,1024]{2,0,1:T(8,128)(2,1)}), bf16[5,512,1024]{2,0,1:T(8,128)(2,1)}, u32[]{:S(2)}, u32[]{:S(2)}) async-start(bf16[5,512,1024]{2,0,1:T(8,128)(2,1)} %scatter_fusion), calls=%async_computation.1 | async-start | bytes 16777216 | tf_op jit(solution)/shard_map/all_to_all | solution.py:198
  227.3 2.2 slice-start
  229.5 3.0 copy-start.23
  247.9 2.2 slice-start.1
  408.7 14.2 %copy-start.9 = (bf16[256,1024]{1,0:T(8,128)(2,1)S(1)}, bf16[256,1024]{1,0:T(8,128)(2,1)}, u32[]{:S(2)}) copy-start(bf16[256,1024]{1,0:T(8,128)(2,1)} %param.17) | copy-start | bytes 1572868
  422.9 6.9 copy-start.2
  422.9 9.5 %copy-start.4 = (f32[1,256,1024]{2,0,1:T(1,128)}, f32[1,256,1024]{2,0,1:T(1,128)S(1)}, u32[]{:S(2)}) copy-start(f32[1,256,1024]{2,0,1:T(1,128)S(1)} %get-tuple-element.409) | copy-start | bytes 3145732
  423.2 9.2 collective-permute-start
  425.0 7.4 copy-start.6
  425.0 22.8 %collective-permute-start.1 = (bf16[8,1024]{1,0:T(8,128)(2,1)S(1)}, bf16[8,1024]{1,0:T(8,128)(2,1)S(1)}, u32[]{:S(2)}, u32[]{:S(2)}) collective-permute-start(bf16[8,1024]{1,0:T(8,128)(2,1)S(1)} %slice.236), channel_id=1, source_target_pairs={{0,8},{8,16},{16,24},{24,32},{32,40},{40,48},{48,56},{56,64},{64,7... | collective-permute-start | bytes 49160 | tf_op jit(solution)/shard_map/ppermute | solution.py:10
  447.8 8.1 copy-start
  447.8 8.1 copy-start.7
  447.8 8.1 copy-start.11
  447.8 8.1 copy-start.12
  447.8 8.1 copy-start.13
  447.8 8.1 copy-start.14
  447.9 8.1 copy-start.15
  454.2 10.8 %copy-start.5 = (f32[1,256,1024]{2,0,1:T(1,128)S(1)}, f32[1,256,1024]{2,0,1:T(1,128)}, u32[]{:S(2)}) copy-start(f32[1,256,1024]{2,0,1:T(1,128)} %copy-done.4) | copy-start | bytes 3145732
  454.2 10.8 %copy-start.16 = (pred[256]{0:T(512)(128)(4,1)S(1)}, pred[256]{0:T(512)(128)(4,1)}, u32[]{:S(2)}) copy-start(pred[256]{0:T(512)(128)(4,1)} %get-tuple-element.422) | copy-start | bytes 772
  454.2 10.8 %copy-start.17 = (pred[256]{0:T(512)(128)(4,1)S(1)}, pred[256]{0:T(512)(128)(4,1)}, u32[]{:S(2)}) copy-start(pred[256]{0:T(512)(128)(4,1)} %get-tuple-element.423) | copy-start | bytes 772
  454.2 10.8 %copy-start.18 = (pred[256]{0:T(512)(128)(4,1)S(1)}, pred[256]{0:T(512)(128)(4,1)}, u32[]{:S(2)}) copy-start(pred[256]{0:T(512)(128)(4,1)} %get-tuple-element.424) | copy-start | bytes 772
  454.3 10.8 %copy-start.19 = (pred[256]{0:T(512)(128)(4,1)S(1)}, pred[256]{0:T(512)(128)(4,1)}, u32[]{:S(2)}) copy-start(pred[256]{0:T(512)(128)(4,1)} %get-tuple-element.425) | copy-start | bytes 772
  454.3 10.8 %copy-start.20 = (pred[256]{0:T(512)(128)(4,1)S(1)}, pred[256]{0:T(512)(128)(4,1)}, u32[]{:S(2)}) copy-start(pred[256]{0:T(512)(128)(4,1)} %get-tuple-element.426) | copy-start | bytes 772
  454.3 10.8 %copy-start.21 = (pred[256]{0:T(512)(128)(4,1)S(1)}, pred[256]{0:T(512)(128)(4,1)}, u32[]{:S(2)}) copy-start(pred[256]{0:T(512)(128)(4,1)} %get-tuple-element.427) | copy-start | bytes 772
  454.3 10.8 %copy-start.22 = (pred[256]{0:T(512)(128)(4,1)S(1)}, pred[256]{0:T(512)(128)(4,1)}, u32[]{:S(2)}) copy-start(pred[256]{0:T(512)(128)(4,1)} %get-tuple-element.428) | copy-start | bytes 772
  454.3 13.6 %copy-start.3 = (f32[1,256,1024]{2,0,1:T(1,128)S(1)}, f32[1,256,1024]{2,0,1:T(1,128)}, u32[]{:S(2)}) copy-start(f32[1,256,1024]{2,0,1:T(1,128)} %copy-done.2) | copy-start | bytes 3145732
  454.3 13.9 %collective-permute-start.3 = (bf16[128,1024]{1,0:T(8,128)(2,1)S(1)}, bf16[128,1024]{1,0:T(8,128)(2,1)S(1)}, u32[]{:S(2)}, u32[]{:S(2)}) collective-permute-start(bf16[128,1024]{1,0:T(8,128)(2,1)S(1)} %slice.259), channel_id=1, source_target_pairs={{0,8},{8,16},{16,24},{24,32},{32,40},{40,48},{48,56},{56,64},{64,7... | collective-permute-start | bytes 786440 | tf_op jit(solution)/shard_map/ppermute | solution.py:10
  458.0 7.0 collective-permute-start.2
  468.2 1.5 copy-start.8
  529.2 15.3 %copy-start.1 = (bf16[1,256,1024]{2,0,1:T(2,128)(2,1)S(1)}, bf16[1,256,1024]{2,0,1:T(2,128)(2,1)}, u32[]{:S(2)}) copy-start(bf16[1,256,1024]{2,0,1:T(2,128)(2,1)} %get-tuple-element.410) | copy-start | bytes 1572868
  529.2 194.6 %all-to-all-start.2 = ((bf16[5,512,1024]{2,0,1:T(8,128)(2,1)}), bf16[5,512,1024]{2,0,1:T(8,128)(2,1)}, u32[]{:S(2)}, u32[]{:S(2)}) async-start(bf16[5,512,1024]{2,0,1:T(8,128)(2,1)} %scatter_fusion.1), calls=%async_computation.2 | async-start | bytes 16777216 | tf_op jit(solution)/shard_map/all_to_all | solution.py:260
  730.0 202.0 %all-to-all-start.3 = ((bf16[5,256,1024]{2,0,1:T(8,128)(2,1)}), bf16[5,256,1024]{2,0,1:T(8,128)(2,1)}, u32[]{:S(2)}, u32[]{:S(2)}) async-start(bf16[5,256,1024]{2,0,1:T(8,128)(2,1)} %bitcast.212), calls=%async_computation.3 | async-start | bytes 8388608 | tf_op jit(solution)/shard_map/all_to_all | solution.py:262
where the time goes:
time: 948 us; the launch traced here: 939 us
  waiting for transfers between devices  287 us (30%)
  local copies, waits for them, and re-layouts  281 us (30%)
  blocking collectives  242 us (26%)
  other arithmetic  48.8 us (5%)
  starting transfers between devices  48.4 us (5%)
  matrix products  26.1 us (3%)
    all_to_all x1, waiting for transfers between devices, on_device(): lax.all_to_all(outbound, 'dp', split_axis=1, concat_axis=1, tiled=True)  162 us
    psum x1, blocking collectives, on_device(): short_total, long_total = lax.psum((short_part, long_part), 'dp')  142 us
    all_to_all x1, waiting for transfers between devices, on_device(): lax.all_to_all(parcels, 'dp', split_axis=1, concat_axis=1, tiled=True)  117 us
    unnamed x1, blocking collectives  99.3 us
    unnamed x63, local copies, waits for them, and re-layouts  57.5 us
    scatter x1, local copies, waits for them, and re-layouts, on_device(): parcels = jnp.zeros((columns.shape[0], shards * capacity, channels), jnp....  33.6 us
    scatter x1, local copies, waits for them, and re-layouts, on_device(): outbound = jnp.zeros((returning.shape[0], shards * capacity, channels), j...  33.5 us
    scatter x1, local copies, waits for them, and re-layouts, on_device(): source_of = jnp.zeros((local_rows,), jnp.int32).at[landing.reshape(-1)].s...  30.4 us
  transfers between devices with their start and end apart: 8, of which 4 were waited for; matrix products, arithmetic and copies ran while one was open for 16% of the time, Pallas kernels for 0%

commit v1 on v0

--- a/solution.py
+++ b/solution.py
@@ -2,6 +2,22 @@
 import jax.numpy as jnp
 from jax import lax
 from jax.sharding import PartitionSpec as P
+
+
+def exchange_in_pairs(x, axis, split, join):
+    ways, here = (lax.axis_size(axis), lax.axis_index(axis))
+    width = x.shape[split] // ways
+    dims = list(x.shape)
+    dims[split] = width
+    height = dims[join]
+    dims[join] = height * ways
+    full = jnp.zeros(dims, x.dtype)
+    for mask in range(ways):
+        part = lax.dynamic_slice_in_dim(x, (here ^ mask) * width, width, axis=split)
+        if mask:
+            part = lax.ppermute(part, axis, [(d, d ^ mask) for d in range(ways)])
+        full = lax.dynamic_update_slice_in_dim(full, part, (here ^ mask) * height, axis=join)
+    return full
 
 
 def shifted(shard, axis, by):
@@ -189,7 +205,7 @@
         .at[landing.reshape(-1)]
         .set(sent_from.reshape(-1), mode="drop")
     )
-    columns = lax.all_to_all(loaded, "mp", split_axis=2, concat_axis=1, tiled=True)
+    columns = exchange_in_pairs(loaded, "mp", 2, 1)
     parcels = (
         jnp.zeros((columns.shape[0], shards * capacity, channels), jnp.bfloat16)
         .at[:, packed_at, :]

time: 948 us -> 913 us (0.963)
  local copies, waits for them, and re-layouts: 281 us -> 238 us
  starting transfers between devices: 48.4 us -> 72 us
  blocking collectives: 242 us -> 229 us
    unnamed x63 -> x68, local copies, waits for them, and re-layouts: 57.5 us -> 15.8 us
    all_to_all x1 -> x0, local copies, waits for them, and re-layouts: 19.8 us -> none  [on_device(): lax.all_to_all(loaded, 'mp', split_axis=2, concat_axis=1, tiled=True)]
    ppermute x4, starting transfers between devices: 8.9 us -> 26 us  [shifted(): return lax.ppermute(shard, axis, pairs)]
    dynamic_update_slice x0 -> x8, local copies, waits for them, and re-layouts: none -> 10.9 us  [exchange_in_pairs(): lax.dynamic_update_slice_in_dim(full, part, (here ^ mask) * height, axis=...]
    unnamed x1, blocking collectives: 99.3 us -> 88.8 us
  transfers between devices with their start and end apart: 8 -> 14, of which waited for: 4 -> 5; matrix products, arithmetic and copies ran while one was open for 16% -> 19% of each run, Pallas kernels for 0% -> 0%
where the time goes in v1:
time: 913 us; the launch traced here: 904 us
  waiting for transfers between devices  283 us (31%)
  local copies, waits for them, and re-layouts  238 us (26%)
  blocking collectives  229 us (25%)
  starting transfers between devices  72 us (8%)
  other arithmetic  49 us (5%)
  matrix products  26.3 us (3%)
    all_to_all x1, waiting for transfers between devices, on_device(): lax.all_to_all(outbound, 'dp', split_axis=1, concat_axis=1, tiled=True)  162 us
    psum x1, blocking collectives, on_device(): short_total, long_total = lax.psum((short_part, long_part), 'dp')  140 us
    all_to_all x1, waiting for transfers between devices, on_device(): lax.all_to_all(parcels, 'dp', split_axis=1, concat_axis=1, tiled=True)  115 us
    unnamed x1, blocking collectives  88.8 us
    scatter x1, local copies, waits for them, and re-layouts, on_device(): parcels = jnp.zeros((columns.shape[0], shards * capacity, channels), jnp....  33.7 us
    scatter x1, local copies, waits for them, and re-layouts, on_device(): outbound = jnp.zeros((returning.shape[0], shards * capacity, channels), j...  33.6 us
    scatter x1, local copies, waits for them, and re-layouts, on_device(): source_of = jnp.zeros((local_rows,), jnp.int32).at[landing.reshape(-1)].s...  30.4 us
    another operation x4, local copies, waits for them, and re-layouts, band_tiles(): repeated = jnp.tile(head_row, (1, tap_count))  28.1 us
  transfers between devices with their start and end apart: 14, of which 5 were waited for; matrix products, arithmetic and copies ran while one was open for 19% of the time, Pallas kernels for 0%

profile of v1, /device:TPU:4, one launch (start us, length us, event | category | flops | bytes accessed | tf_op | source)
XLA Modules:
  0.0 903.6 jit_solution(7004213431292774063)
XLA Ops:
  0.7 2.0 constant_dynamic-slice_fusion.4
  2.8 3.0 collective-permute-start.4
  6.6 2.9 collective-permute-start.1
  9.7 88.8 %all-reduce.2 = s32[8192]{0:T(1024)S(1)} all-reduce(s32[8192]{0:T(1024)S(1)} %dynamic-update-slice), channel_id=1, replica_groups=mesh['dp'=32,'mp'=8] {'dp','mp'}, use_global_device_ids=true, to_apply=%add.2 | all-reduce | flops 8192 | bytes 65536
  99.6 2.5 broadcast_in_dim.252
  103.2 1.5 collective-permute-start.2
  104.7 2.0 copy_dynamic-update-slice_fusion.6
  107.4 2.0 copy_dynamic-update-slice_fusion.5
  109.3 3.6 collective-permute-done.2
  113.9 2.0 copy_dynamic-update-slice_fusion.3
  118.9 4.3 broadcast.301.clone
  123.2 33.7 %scatter_fusion = bf16[5,512,1024]{2,0,1:T(8,128)(2,1)} fusion(bf16[5,512,1024]{2,0,1:T(8,128)(2,1)} %broadcast.301.clone, s32[256]{0:T(256)S(1)} %compare_select_fusion.1, bf16[256,5,1024]{2,1,0:T(8,128)(2,1)} %bitcast.12), kind=kCustom, calls=%fused_computation.3 | custom fusion | bytes 7865344 | tf_op jit(solution)/shard_map/scatter | solution.py:212
  156.9 6.6 all-to-all-start
  166.1 3.2 tile.8
  169.3 10.8 %tile.9 = bf16[64,32896]{1,0:T(8,128)(2,1)} reshape(bf16[64,128,257]{2,1,0:T(8,128)(2,1)} %tile.8) | data formatting | bytes 8421376 | tf_op jit(solution)/shard_map/tile | solution.py:51
  180.1 2.2 slice-done
  182.3 3.0 copy.137
  185.4 3.2 tile.20
  188.7 10.8 %tile.21 = bf16[64,32896]{1,0:T(8,128)(2,1)} reshape(bf16[64,128,257]{2,1,0:T(8,128)(2,1)} %tile.20) | data formatting | bytes 8421376 | tf_op jit(solution)/shard_map/tile | solution.py:51
  199.5 2.2 slice-done.1
  201.7 3.0 copy.138
  204.7 30.4 %scatter_custom_fusion = s32[256]{0:T(256)S(1)} fusion(s32[8192]{0:T(1024)S(1)} %get-tuple-element.401, s32[8192]{0:T(1024)S(1)} %get-tuple-element.400, s32[]{:T(128)} %copy.226), kind=kCustom, calls=%fused_computation.222 | custom fusion | bytes 1028 | tf_op jit(solution)/shard_map/scatter | solution.py:206
  236.6 115.3 %all-to-all-done = bf16[5,512,1024]{2,0,1:T(8,128)(2,1)} async-done(((bf16[5,512,1024]{2,0,1:T(8,128)(2,1)}), bf16[5,512,1024]{2,0,1:T(8,128)(2,1)}, u32[]{:S(2)}, u32[]{:S(2)}) %all-to-all-start) | async-done | bytes 5242912 | tf_op jit(solution)/shard_map/all_to_all | solution.py:214
  352.0 6.2 gather_fusion
  358.1 14.2 %slice_convert_fusion.1 = (f32[1,256,1024]{2,0,1:T(1,128)S(1)}, bf16[1,256,1024]{2,0,1:T(2,128)(2,1)S(1)}, bf16[1,256,1024]{2,0,1:T(2,128)(2,1)S(1)}, f32[1,256,1024]{2,0,1:T(1,128)S(1)}, bf16[1,256,1024]{2,0,1:T(2,128)(2,1)}) fusion(bf16[5,256,1024]{2,0,1:T(8,128)(2,1)} %bitcast.201), kind=kLoop, calls=%fused_computation.93 | loop fusion | flops 524288 | bytes 6291456 | tf_op jit(solution)/shard_map/convert_element_type | solution.py:221
  372.7 1.3 collective-permute-start.7
  374.5 18.7 %collective-permute-start.8 = (bf16[8,1024]{1,0:T(8,128)(2,1)S(1)}, bf16[8,1024]{1,0:T(8,128)(2,1)S(1)}, u32[]{:S(2)}, u32[]{:S(2)}) collective-permute-start(bf16[8,1024]{1,0:T(8,128)(2,1)S(1)} %slice.236), channel_id=1, source_target_pairs={{0,8},{8,16},{16,24},{24,32},{32,40},{40,48},{48,56},{56,64},{64,7... | collective-permute-start | bytes 49160 | tf_op jit(solution)/shard_map/ppermute | solution.py:26
  393.8 13.5 %while.38 = (s32[]{:T(128)}, f32[2,128,1024]{1,2,0:T(8,128)}, s32[2]{0:T(128)}, bf16[384,1024]{1,0:T(8,128)(2,1)S(1)}, s32[]{:T(128)}, /*index=5*/s32[384]{0:T(512)S(1)}, bf16[64,128,256]{2,1,0:T(8,128)(2,1)}, s32[1]{0:T(128)}) while((s32[]{:T(128)}, f32[2,128,1024]{1,2,0:T(8,128)}, s32[2]{0:T(128)}, ...), condition=%wide.region_10.11_spmd.clone, body=%wide.region_9.10_spmd.sunk.clone | while | flops 69271688 | bytes 16912620 | solution.py:150
  396.0 3.5 fusion.106
  402.8 3.5 fusion.106
  407.3 2.6 copy.97
  410.0 5.4 fusion.43
  416.8 2.6 fusion.23
  419.9 4.7 collective-permute-start.10
  424.9 2.8 fusion.52
  428.0 1.8 collective-permute-done.10
  430.2 11.9 %while.39 = (s32[]{:T(128)}, f32[2,128,1024]{2,1,0:T(8,128)}, s32[2]{0:T(128)S(1)}, bf16[384,1024]{0,1:T(8,128)(2,1)S(1)}, s32[]{:T(128)}, /*index=5*/s32[256]{0:T(256)S(1)}, bf16[64,128,256]{2,1,0:T(8,128)(2,1)}, s32[1]{0:T(128)}) while((s32[]{:T(128)}, f32[2,128,1024]{2,1,0:T(8,128)}, s32[2]{0:T(128)S(1)}, ...), condition=%wide.region_13.14_spmd.clone, body=%wide.region_12.13_spmd.sunk.clone | while | flops 69271816 | bytes 8523480 | solution.py:123
  431.7 3.4 fusion.109
  437.6 3.4 fusion.109
  442.1 2.3 bitcast_dynamic-update-slice_fusion.1
  444.4 1.9 bitcast_dynamic-update-slice_fusion
  446.2 5.3 copy.102
  451.5 4.3 broadcast.301
  455.8 33.6 %scatter_fusion.1 = bf16[5,512,1024]{2,0,1:T(8,128)(2,1)} fusion(bf16[5,512,1024]{2,0,1:T(8,128)(2,1)} %broadcast.301, s32[256]{0:T(256)S(1)} %compare_select_fusion.2, bf16[256,5,1024]{2,1,0:T(8,128)(2,1)} %copy.102), kind=kCustom, calls=%fused_computation.4 | custom fusion | bytes 7865344 | tf_op jit(solution)/shard_map/scatter | solution.py:274
  489.4 20.1 %all-to-all-start.1 = ((bf16[5,512,1024]{2,0,1:T(8,128)(2,1)}), bf16[5,512,1024]{2,0,1:T(8,128)(2,1)}, u32[]{:S(2)}, u32[]{:S(2)}) async-start(bf16[5,512,1024]{2,0,1:T(8,128)(2,1)} %scatter_fusion.1), calls=%async_computation.1 | async-start | bytes 16777216 | tf_op jit(solution)/shard_map/all_to_all | solution.py:276
  509.6 5.7 convert_convert_fusion
  516.4 2.6 copy.106
  519.1 1.8 copy_convert_fusion
  520.9 2.7 copy.105
  523.5 2.5 copy.104
  527.3 1.8 select_reduce_fusion
  529.3 162.0 %all-to-all-done.1 = bf16[5,512,1024]{2,0,1:T(8,128)(2,1)} async-done(((bf16[5,512,1024]{2,0,1:T(8,128)(2,1)}), bf16[5,512,1024]{2,0,1:T(8,128)(2,1)}, u32[]{:S(2)}, u32[]{:S(2)}) %all-to-all-start.1) | async-done | bytes 5242912 | tf_op jit(solution)/shard_map/all_to_all | solution.py:276
  691.3 6.2 gather_fusion.1
  697.5 10.4 %all-to-all-start.2 = ((bf16[5,256,1024]{2,0,1:T(8,128)(2,1)}), bf16[5,256,1024]{2,0,1:T(8,128)(2,1)}, u32[]{:S(2)}, u32[]{:S(2)}) async-start(bf16[5,256,1024]{2,0,1:T(8,128)(2,1)} %bitcast.205), calls=%async_computation.2 | async-start | bytes 8388608 | tf_op jit(solution)/shard_map/all_to_all | solution.py:278
  707.9 16.0 %while.40 = (s32[]{:T(128)}, f32[64,128,256]{2,1,0:T(8,128)}, s32[2]{0:T(128)S(1)}, bf16[256,1024]{1,0:T(8,128)(2,1)S(1)}, bf16[384,1024]{0,1:T(8,128)(2,1)S(1)}, /*index=5*/s32[]{:T(128)}, s32[256]{0:T(256)S(1)}, s32[1]{0:T(128)}) while((s32[]{:T(128)}, f32[64,128,256]{2,1,0:T(8,128)}, s32[2]{0:T(128)S(1)}, ...), condition=%wide.region_31.32_spmd.clone.clone, body=%wide.region_30.31_spmd.clone.sunk.clone | while | flops 73466120 | bytes 19926752 | solution.py:176
  709.6 4.6 select_add_fusion.3
  715.9 8.0 select_add_fusion.3
  723.9 8.1 copy.139
  732.0 3.8 concatenate.27
  735.7 14.1 %reshape.378 = f32[64,128,257]{2,1,0:T(8,128)} reshape(f32[64,32896]{1,0:T(8,128)} %concatenate.27) | data formatting | bytes 16842752 | tf_op jit(solution)/shard_map/reshape | solution.py:61
  749.9 4.5 slice_reduce_fusion
  754.5 140.5 %all-reduce.3 = (f32[7,64]{1,0:T(8,128)S(1)}, f32[128,64]{0,1:T(8,128)S(1)}) all-reduce(f32[7,64]{1,0:T(8,128)S(1)} %stack.55, f32[128,64]{0,1:T(8,128)S(1)} %bitcast.213), channel_id=1, replica_groups=mesh['dp'=32,'mp'=8] {'dp'}, use_global_device_ids=true, to_apply=%region_29.30 | all-reduce | flops 8640 | bytes 69120 | tf_op jit(solution)/shard_map/psum | solution.py:260
  896.2 3.9 copy.103
  900.1 3.1 all_to_all.24
  (224 shorter events, 31.1 us)
Async XLA Ops:
  0.6 8.8 copy-start.31
  2.7 115.3 %collective-permute-start.6 = (bf16[5,32,1024]{2,1,0:T(8,128)(2,1)S(1)}, bf16[5,32,1024]{2,1,0:T(8,128)(2,1)S(1)}, u32[]{:S(2)}, u32[]{:S(2)}) collective-permute-start(bf16[5,32,1024]{2,1,0:T(8,128)(2,1)S(1)} %get-tuple-element.390), channel_id=1, source_target_pairs={{0,7},{1,6},{2,5},{3,4},{4,3},{5,2},{6,1},{7,0},{8,15},{9,14},{10,... | collective-permute-start | bytes 983048 | tf_op jit(solution)/shard_map/ppermute | solution.py:18
  2.8 113.1 %collective-permute-start.4 = (bf16[5,32,1024]{2,1,0:T(8,128)(2,1)S(1)}, bf16[5,32,1024]{2,1,0:T(8,128)(2,1)S(1)}, u32[]{:S(2)}, u32[]{:S(2)}) collective-permute-start(bf16[5,32,1024]{2,1,0:T(8,128)(2,1)S(1)} %get-tuple-element.391), channel_id=1, source_target_pairs={{0,5},{1,4},{2,7},{3,6},{4,1},{5,0},{6,3},{7,2},{8,13},{9,12},{10,... | collective-permute-start | bytes 983048 | tf_op jit(solution)/shard_map/ppermute | solution.py:18
  5.8 108.1 %collective-permute-start.3 = (bf16[5,32,1024]{2,1,0:T(8,128)(2,1)S(1)}, bf16[5,32,1024]{2,1,0:T(8,128)(2,1)}, u32[]{:S(2)}, u32[]{:S(2)}) collective-permute-start(bf16[5,32,1024]{2,1,0:T(8,128)(2,1)S(1)} %get-tuple-element.392), channel_id=1, source_target_pairs={{0,4},{1,5},{2,6},{3,7},{4,0},{5,1},{6,2},{7,3},{8,12},{9,13},{10,... | collective-permute-start | bytes 983048 | tf_op jit(solution)/shard_map/ppermute | solution.py:18
  6.6 100.1 %collective-permute-start.1 = (bf16[5,32,1024]{2,1,0:T(8,128)(2,1)S(1)}, bf16[5,32,1024]{2,1,0:T(8,128)(2,1)}, u32[]{:S(2)}, u32[]{:S(2)}) collective-permute-start(bf16[5,32,1024]{2,1,0:T(8,128)(2,1)S(1)} %get-tuple-element.394), channel_id=1, source_target_pairs={{0,2},{1,3},{2,0},{3,1},{4,6},{5,7},{6,4},{7,5},{8,10},{9,11},{10,... | collective-permute-start | bytes 983048 | tf_op jit(solution)/shard_map/ppermute | solution.py:18
  9.4 93.8 %collective-permute-start = (bf16[5,32,1024]{2,1,0:T(8,128)(2,1)S(1)}, bf16[5,32,1024]{2,1,0:T(8,128)(2,1)}, u32[]{:S(2)}, u32[]{:S(2)}) collective-permute-start(bf16[5,32,1024]{2,1,0:T(8,128)(2,1)S(1)} %get-tuple-element.395), channel_id=1, source_target_pairs={{0,1},{1,0},{2,3},{3,2},{4,5},{5,4},{6,7},{7,6},{8,9},{9,8},{10,11... | collective-permute-start | bytes 983048 | tf_op jit(solution)/shard_map/ppermute | solution.py:18
  103.2 9.7 %collective-permute-start.2 = (bf16[5,32,1024]{2,1,0:T(8,128)(2,1)S(1)}, bf16[5,32,1024]{2,1,0:T(8,128)(2,1)S(1)}, u32[]{:S(2)}, u32[]{:S(2)}) collective-permute-start(bf16[5,32,1024]{2,1,0:T(8,128)(2,1)S(1)} %get-tuple-element.393), channel_id=1, source_target_pairs={{0,3},{1,2},{2,1},{3,0},{4,7},{5,6},{6,5},{7,4},{8,11},{9,10},{10,... | collective-permute-start | bytes 983048 | tf_op jit(solution)/shard_map/ppermute | solution.py:18
  106.7 10.3 %collective-permute-start.5 = (bf16[5,32,1024]{2,1,0:T(8,128)(2,1)S(1)}, bf16[5,32,1024]{2,1,0:T(8,128)(2,1)S(1)}, u32[]{:S(2)}, u32[]{:S(2)}) collective-permute-start(bf16[5,32,1024]{2,1,0:T(8,128)(2,1)S(1)} %get-tuple-element.397), channel_id=1, source_target_pairs={{0,6},{1,7},{2,4},{3,5},{4,2},{5,3},{6,0},{7,1},{8,14},{9,15},{10,... | collective-permute-start | bytes 983048 | tf_op jit(solution)/shard_map/ppermute | solution.py:18
  156.9 6.6 copy-start.30
  156.9 6.9 copy-start.29
  156.9 6.9 copy-start.15
  156.9 195.0 %all-to-all-start = ((bf16[5,512,1024]{2,0,1:T(8,128)(2,1)}), bf16[5,512,1024]{2,0,1:T(8,128)(2,1)}, u32[]{:S(2)}, u32[]{:S(2)}) async-start(bf16[5,512,1024]{2,0,1:T(8,128)(2,1)} %scatter_fusion), calls=%async_computation | async-start | bytes 16777216 | tf_op jit(solution)/shard_map/all_to_all | solution.py:214
  180.1 2.2 slice-start
  199.5 2.2 slice-start.1
  358.1 14.2 %copy-start.14 = (bf16[256,1024]{1,0:T(8,128)(2,1)S(1)}, bf16[256,1024]{1,0:T(8,128)(2,1)}, u32[]{:S(2)}) copy-start(bf16[256,1024]{1,0:T(8,128)(2,1)} %param.17) | copy-start | bytes 1572868
  372.3 20.9 %copy-start.3 = (f32[1,256,1024]{2,0,1:T(1,128)}, f32[1,256,1024]{2,0,1:T(1,128)S(1)}, u32[]{:S(2)}) copy-start(f32[1,256,1024]{2,0,1:T(1,128)S(1)} %get-tuple-element.385) | copy-start | bytes 3145732
  372.3 20.9 %copy-start.5 = (f32[1,256,1024]{2,0,1:T(1,128)}, f32[1,256,1024]{2,0,1:T(1,128)S(1)}, u32[]{:S(2)}) copy-start(f32[1,256,1024]{2,0,1:T(1,128)S(1)} %get-tuple-element.388) | copy-start | bytes 3145732
  372.7 20.5 %collective-permute-start.7 = (bf16[128,1024]{1,0:T(8,128)(2,1)S(1)}, bf16[128,1024]{1,0:T(8,128)(2,1)S(1)}, u32[]{:S(2)}, u32[]{:S(2)}) collective-permute-start(bf16[128,1024]{1,0:T(8,128)(2,1)S(1)} %slice.231), channel_id=1, source_target_pairs={{8,0},{16,8},{24,16},{32,24},{40,32},{48,40},{56,48},{64,56},{72,6... | collective-permute-start | bytes 786440 | tf_op jit(solution)/shard_map/ppermute | solution.py:26
  374.4 18.8 %copy-start.7 = (bf16[256,1024]{1,0:T(8,128)(2,1)}, bf16[256,1024]{1,0:T(8,128)(2,1)S(1)}, u32[]{:S(2)}) copy-start(bf16[256,1024]{1,0:T(8,128)(2,1)S(1)} %fusion.44) | copy-start | bytes 1572868
  374.5 35.5 %collective-permute-start.8 = (bf16[8,1024]{1,0:T(8,128)(2,1)S(1)}, bf16[8,1024]{1,0:T(8,128)(2,1)S(1)}, u32[]{:S(2)}, u32[]{:S(2)}) collective-permute-start(bf16[8,1024]{1,0:T(8,128)(2,1)S(1)} %slice.236), channel_id=1, source_target_pairs={{0,8},{8,16},{16,24},{24,32},{32,40},{40,48},{48,56},{56,64},{64,7... | collective-permute-start | bytes 49160 | tf_op jit(solution)/shard_map/ppermute | solution.py:26
  396.0 3.5 copy-start.9
  399.6 1.0 copy-start.10
  402.8 3.5 copy-start.9
  406.3 1.0 copy-start.10
  407.3 9.5 %copy-start = (bf16[1,256,1024]{2,0,1:T(2,128)(2,1)S(1)}, bf16[1,256,1024]{2,0,1:T(2,128)(2,1)}, u32[]{:S(2)}) copy-start(bf16[1,256,1024]{2,0,1:T(2,128)(2,1)} %get-tuple-element.389) | copy-start | bytes 1572868
  407.3 9.5 %copy-start.8 = (bf16[256,1024]{1,0:T(8,128)(2,1)S(1)}, bf16[256,1024]{1,0:T(8,128)(2,1)}, u32[]{:S(2)}) copy-start(bf16[256,1024]{1,0:T(8,128)(2,1)} %copy-done.7) | copy-start | bytes 1572868
  407.3 9.5 %copy-start.16 = (pred[256]{0:T(512)(128)(4,1)S(1)}, pred[256]{0:T(512)(128)(4,1)}, u32[]{:S(2)}) copy-start(pred[256]{0:T(512)(128)(4,1)} %get-tuple-element.418) | copy-start | bytes 772
  407.3 9.5 %copy-start.17 = (pred[256]{0:T(512)(128)(4,1)S(1)}, pred[256]{0:T(512)(128)(4,1)}, u32[]{:S(2)}) copy-start(pred[256]{0:T(512)(128)(4,1)} %get-tuple-element.419) | copy-start | bytes 772
  407.3 9.5 %copy-start.18 = (pred[256]{0:T(512)(128)(4,1)S(1)}, pred[256]{0:T(512)(128)(4,1)}, u32[]{:S(2)}) copy-start(pred[256]{0:T(512)(128)(4,1)} %get-tuple-element.420) | copy-start | bytes 772
  407.3 9.5 %copy-start.19 = (pred[256]{0:T(512)(128)(4,1)S(1)}, pred[256]{0:T(512)(128)(4,1)}, u32[]{:S(2)}) copy-start(pred[256]{0:T(512)(128)(4,1)} %get-tuple-element.421) | copy-start | bytes 772
  407.3 9.5 %copy-start.20 = (pred[256]{0:T(512)(128)(4,1)S(1)}, pred[256]{0:T(512)(128)(4,1)}, u32[]{:S(2)}) copy-start(pred[256]{0:T(512)(128)(4,1)} %get-tuple-element.422) | copy-start | bytes 772
  407.3 9.5 %copy-start.28 = (pred[256]{0:T(512)(128)(4,1)S(1)}, pred[256]{0:T(512)(128)(4,1)}, u32[]{:S(2)}) copy-start(pred[256]{0:T(512)(128)(4,1)} %get-tuple-element.416) | copy-start | bytes 772
  410.0 6.9 copy-start.2
  415.4 9.3 %collective-permute-start.9 = (bf16[8,1024]{1,0:T(8,128)(2,1)S(1)}, bf16[8,1024]{1,0:T(8,128)(2,1)S(1)}, u32[]{:S(2)}, u32[]{:S(2)}) collective-permute-start(bf16[8,1024]{1,0:T(8,128)(2,1)S(1)} %slice.248), channel_id=1, source_target_pairs={{8,0},{16,8},{24,16},{32,24},{40,32},{48,40},{56,48},{64,56},{72,6... | collective-permute-start | bytes 49160 | tf_op jit(solution)/shard_map/ppermute | solution.py:26
  419.4 5.4 copy-start.6
  419.4 5.4 copy-start.21
  419.4 5.4 copy-start.22
  419.4 5.4 copy-start.23
  419.4 5.4 copy-start.24
  419.5 5.4 copy-start.25
  419.5 5.4 copy-start.26
  419.5 5.4 copy-start.27
  419.5 8.2 copy-start.4
  419.9 9.9 %collective-permute-start.10 = (bf16[128,1024]{1,0:T(8,128)(2,1)S(1)}, bf16[128,1024]{1,0:T(8,128)(2,1)S(1)}, u32[]{:S(2)}, u32[]{:S(2)}) collective-permute-start(bf16[128,1024]{1,0:T(8,128)(2,1)S(1)} %slice.259), channel_id=1, source_target_pairs={{0,8},{8,16},{16,24},{24,32},{32,40},{40,48},{48,56},{56,64},{64,7... | collective-permute-start | bytes 786440 | tf_op jit(solution)/shard_map/ppermute | solution.py:26
  428.0 1.8 copy-start.13
  489.4 201.9 %all-to-all-start.1 = ((bf16[5,512,1024]{2,0,1:T(8,128)(2,1)}), bf16[5,512,1024]{2,0,1:T(8,128)(2,1)}, u32[]{:S(2)}, u32[]{:S(2)}) async-start(bf16[5,512,1024]{2,0,1:T(8,128)(2,1)} %scatter_fusion.1), calls=%async_computation.1 | async-start | bytes 16777216 | tf_op jit(solution)/shard_map/all_to_all | solution.py:276
  509.5 9.5 %copy-start.1 = (bf16[1,256,1024]{2,0,1:T(2,128)(2,1)S(1)}, bf16[1,256,1024]{2,0,1:T(2,128)(2,1)}, u32[]{:S(2)}) copy-start(bf16[1,256,1024]{2,0,1:T(2,128)(2,1)} %get-tuple-element.389) | copy-start | bytes 1572868
  520.9 6.4 copy-start.11
  520.9 6.4 copy-start.12
  697.5 198.7 %all-to-all-start.2 = ((bf16[5,256,1024]{2,0,1:T(8,128)(2,1)}), bf16[5,256,1024]{2,0,1:T(8,128)(2,1)}, u32[]{:S(2)}, u32[]{:S(2)}) async-start(bf16[5,256,1024]{2,0,1:T(8,128)(2,1)} %bitcast.205), calls=%async_computation.2 | async-start | bytes 8388608 | tf_op jit(solution)/shard_map/all_to_all | solution.py:278
